TPU v7x, 128 devices: a whole 4x4x4 slice. The times are simulated.
128 devices in a mesh: seq: 32 (over x, z, core), head: 4 (over y).
Axes of the slice: x: 4, y: 4, z: 4, core: 2. Of those that a mesh axis runs over, the one named last changes fastest.
Arguments:
- values: bfloat16 [32768, 8192], P('seq', 'head'), may hold values from -0.0625 to 0.0625
- writes: bfloat16 [32768, 128], P('seq'), may hold values from -0.5 to 0.5
- reads: bfloat16 [32768, 128], P('seq'), may hold values from -0.5 to 0.5
- out_grad: bfloat16 [32768, 8192], P('seq', 'head'), may hold values from -0.375 to 0.375
- log_decay: float32 [128, 32768], P('head', 'seq'), may hold values from -2 to 0, as said below
- starting_head_state: float32 [128, 8192], P('head'), may hold values from -1.5 to 1.5
Outputs:
- values_grad: bfloat16 [32768, 8192], P('seq', 'head')
- writes_grad: float32 [32768, 128], P('seq')
- reads_grad: float32 [32768, 128], P('seq')
- initial_grad: float32 [128, 8192], P('head')
Inputs may be any that keep to these rules, and one draw needn't show every extreme that they name: `log_decay`: each entry is the logarithm of a head's decay factor at a position.
All inputs are finite; a program needn't handle non-finite values.
Results may differ from a plain program's by a relative error of at most 0.0013.
Values sent between devices are 32-bit elements; how exact they have to be, the bound alone decides.
A program may use at most 256 MiB of HBM per device.

v0:
```python
import jax
import jax.numpy as jnp
from jax import lax
from jax.sharding import PartitionSpec as P

HEAD_DIM = 64
D_STATE = 128
highest = lax.Precision.HIGHEST


def carried_in(part, axis, combine, identity, reverse):
    count = lax.axis_size(axis)
    place = lax.axis_index(axis)
    ahead = count - 1 - place if reverse else place
    gathered = jax.tree.map(lambda a: lax.all_gather(a, axis), part)
    state = jax.tree.map(lambda a, e: jnp.zeros_like(a) + jnp.asarray(e, a.dtype), part, identity)

    def one(turn, state):
        source = count - 1 - turn if reverse else turn
        return combine(
            state, jax.tree.map(lambda a: lax.dynamic_index_in_dim(a, source, 0, False), gathered)
        )

    return lax.fori_loop(0, ahead, one, state)


def forward_join(earlier, latter):
    return (earlier[0] + latter[0], jnp.exp(latter[0]) * earlier[1] + latter[1])


def backward_join(earlier, latter):
    return (earlier[0] + latter[0], latter[1] + jnp.exp(latter[0]) * earlier[1])


def per_device(values, writes, reads, out_grad, log_decay, starting_head_state):
    tokens = values.shape[0]
    head_count = log_decay.shape[0]
    block_size = min(512, tokens)
    block_count = tokens // block_size
    state_shape = (head_count, HEAD_DIM, D_STATE)
    flat_size = HEAD_DIM * D_STATE
    causal = lax.broadcasted_iota(jnp.int32, (block_size, block_size), 0) >= lax.broadcasted_iota(
        jnp.int32, (block_size, block_size), 1
    )
    blocks = []
    for block_index in range(block_count):
        first_row = block_index * block_size
        block_values = lax.slice_in_dim(values, first_row, first_row + block_size).reshape(
            block_size, head_count, HEAD_DIM
        )
        block_grads = lax.slice_in_dim(out_grad, first_row, first_row + block_size).reshape(
            block_size, head_count, HEAD_DIM
        )
        block_writes = lax.slice_in_dim(writes, first_row, first_row + block_size)
        block_reads = lax.slice_in_dim(reads, first_row, first_row + block_size)
        block_logs = lax.slice_in_dim(log_decay, first_row, first_row + block_size, axis=1)
        cumulative = jnp.cumsum(block_logs, axis=1)
        block_total = cumulative[:, -1]
        to_end = jnp.exp(block_total[:, None] - cumulative).T[:, :, None]
        from_start = jnp.exp(cumulative).T[:, :, None]
        log_gaps = cumulative[:, :, None] - cumulative[:, None, :]
        decay_mask = jnp.exp(jnp.where(causal[None], log_gaps, -1e30))
        intersections = jnp.einsum(
            "sn,in->si", block_reads, block_writes, preferred_element_type=jnp.float32
        )
        products = jnp.einsum(
            "shp,ihp->hsi", block_grads, block_values, preferred_element_type=jnp.float32
        )
        mixed_sums = jnp.sum(products * decay_mask, axis=0)
        values_wide = block_values.astype(jnp.float32)
        grads_wide = block_grads.astype(jnp.float32)
        writes_wide = block_writes.astype(jnp.float32)
        reads_wide = block_reads.astype(jnp.float32)
        interior_quantities = jnp.einsum(
            "hsi,shp->ihp", intersections[None] * decay_mask, grads_wide, precision=highest
        )
        inner_writes = jnp.einsum("si,sn->in", mixed_sums, reads_wide, precision=highest)
        inner_reads = jnp.einsum("si,in->sn", mixed_sums, writes_wide, precision=highest)
        rescaled_quantities = values_wide * to_end
        scaled_grads = grads_wide * from_start
        fresh_state = jnp.einsum("jhp,jn->hpn", rescaled_quantities, writes_wide, precision=highest)
        carried = jnp.einsum("shp,sn->hpn", scaled_grads, reads_wide, precision=highest)
        blocks.append(
            (
                block_total,
                to_end,
                writes_wide,
                rescaled_quantities,
                scaled_grads,
                interior_quantities,
                inner_writes,
                inner_reads,
                fresh_state,
                carried,
            )
        )
    local_state = jnp.zeros(state_shape, jnp.float32)
    total_log = jnp.zeros((head_count,), jnp.float32)
    for block_index in range(block_count):
        block_total = blocks[block_index][0]
        local_state = jnp.exp(block_total)[:, None, None] * local_state + blocks[block_index][8]
        total_log = total_log + block_total
    local_adjoint = jnp.zeros(state_shape, jnp.float32)
    for block_index in reversed(range(block_count)):
        block_total = blocks[block_index][0]
        local_adjoint = blocks[block_index][9] + jnp.exp(block_total)[:, None, None] * local_adjoint
    local_state = local_state.reshape(head_count, flat_size)
    local_adjoint = local_adjoint.reshape(head_count, flat_size)
    empty = (
        jnp.zeros((head_count, 1), jnp.float32),
        jnp.zeros((head_count, flat_size), jnp.float32),
    )
    prefix_log, prefix_state = carried_in(
        (total_log[:, None], local_state), "seq", forward_join, empty, False
    )
    ignored, after_device = carried_in(
        (total_log[:, None], local_adjoint), "seq", backward_join, empty, True
    )
    entering = prefix_state + jnp.exp(prefix_log) * starting_head_state
    initial_grad = lax.psum(jnp.exp(prefix_log) * local_adjoint, "seq")
    start_state = entering.reshape(state_shape)
    starts = []
    for block_index in range(block_count):
        starts.append(start_state)
        start_state = (
            jnp.exp(blocks[block_index][0])[:, None, None] * start_state + blocks[block_index][8]
        )
    after_end = after_device.reshape(state_shape)
    afters = [after_end] * block_count
    for block_index in reversed(range(block_count)):
        afters[block_index] = after_end
        after_end = (
            blocks[block_index][9] + jnp.exp(blocks[block_index][0])[:, None, None] * after_end
        )
    value_parts = []
    write_parts = []
    read_parts = []
    for block_index in range(block_count):
        (
            block_total,
            to_end,
            writes_wide,
            rescaled_quantities,
            scaled_grads,
            interior_quantities,
            inner_writes,
            inner_reads,
            fresh_state,
            carried,
        ) = blocks[block_index]
        outer_values = (
            jnp.einsum("in,hpn->ihp", writes_wide, afters[block_index], precision=highest) * to_end
        )
        value_parts.append(
            (interior_quantities + outer_values)
            .reshape(block_size, head_count * HEAD_DIM)
            .astype(jnp.bfloat16)
        )
        write_parts.append(
            inner_writes
            + jnp.einsum("ihp,hpn->in", rescaled_quantities, afters[block_index], precision=highest)
        )
        read_parts.append(
            inner_reads
            + jnp.einsum("shp,hpn->sn", scaled_grads, starts[block_index], precision=highest)
        )
    values_grad = jnp.concatenate(value_parts, axis=0)
    writes_local = jnp.concatenate(write_parts, axis=0)
    reads_local = jnp.concatenate(read_parts, axis=0)
    writes_grad, reads_grad = lax.psum((writes_local, reads_local), "head")
    return (values_grad, writes_grad, reads_grad, initial_grad)


def solution(mesh):
    in_specs = (
        P("seq", "head"),
        P("seq", None),
        P("seq", None),
        P("seq", "head"),
        P("head", "seq"),
        P("head", None),
    )
    out_specs = (P("seq", "head"), P("seq", None), P("seq", None), P("head", None))
    return jax.shard_map(
        per_device, mesh=mesh, in_specs=in_specs, out_specs=out_specs, check_vma=False
    )
```

profile of v0, /device:TPU:0, one launch (start us, length us, event | category | flops | bytes accessed | tf_op | source)
XLA Modules:
  0.0 539.7 jit_solution(1974260773346399867)
XLA Ops:
  13.3 4.8 fusion.76
  18.1 2.9 copy.60
  21.1 4.6 copy.53
  25.7 3.8 fusion.27
  29.5 3.9 fusion.38
  33.4 2.4 all_gather_reshape.6
  36.1 4.8 fusion.75
  41.0 4.0 copy.61
  45.0 4.0 copy.58
  48.9 4.0 fusion.21
  53.9 4.8 fusion.41
  61.3 4.3 bitcast_multiply_fusion.1
  65.5 2.6 bitcast_multiply_fusion
  69.7 70.5 %all-reduce = f32[1024]{0:T(1024)S(1)} all-reduce(f32[1024]{0:T(1024)S(1)} %dynamic-update-slice), channel_id=2, replica_groups=mesh['seq'=32,'head'=4] {'seq'}, use_global_device_ids=true, to_apply=%add | all-reduce | flops 1024 | bytes 8192
  144.9 14.0 %multiply_reduce_fusion = f32[512,512]{1,0:T(8,128)} fusion(f32[32,512]{1,0:T(8,128)} %copy-done.28, pred[512,512]{1,0:T(8,128)(4,1)S(1)} %iota_compare_fusion, bf16[512,32,64]{0,2,1:T(8,128)(2,1)} %bitcast.143, bf16[512,32,64]{0,2,1:T(8,128)(2,1)} %bitcast.150), kind=kOutput, calls=%fused_computation.6 | convolution fusion | flops 1107034112 | bytes 5570560 | tf_op jit(solution)/shard_map/shp,ihp->hsi/dot_general | solution.py:66
  158.9 11.7 %multiply_reduce_fusion.1 = f32[512,512]{1,0:T(8,128)} fusion(f32[32,512]{1,0:T(8,128)S(1)} %copy-done.26, pred[512,512]{1,0:T(8,128)(4,1)S(1)} %iota_compare_fusion, bf16[512,32,64]{0,2,1:T(8,128)(2,1)S(1)} %bitcast.140, bf16[512,32,64]{0,2,1:T(8,128)(2,1)S(1)} %bitcast.148), kind=kOutput, calls=%fused_computation.7 | convolution fusion | flops 1107034112 | bytes 5570560 | tf_op jit(solution)/shard_map/shp,ihp->hsi/dot_general | solution.py:66
  170.6 48.5 %while.26 = (s32[]{:T(128)}, f32[32,8192]{1,0:T(8,128)S(1)}, s32[]{:T(128)}, f32[32,32,8192]{2,1,0:T(8,128)}, f32[32,32,1]{1,2,0:T(1,128)S(1)}, /*index=5*/s32[]{:T(128)}, s32[]{:T(128)}, s32[]{:T(128)}, s32[]{:T(128)}) while((s32[]{:T(128)}, f32[32,8192]{1,0:T(8,128)S(1)}, s32[]{:T(128)}, f32[32,32,8192]{2,1,0:T(8,128)}, ...), condition=%wide.region_5.6_spmd, body=%wide.region_4.5_spmd.sunk | while | flops 524294 | bytes 3146267 | solution.py:24
  219.4 9.2 %fusion.45 = f32[512,128]{1,0:T(8,128)} fusion(bf16[512,32,64]{0,2,1:T(8,128)(2,1)} %bitcast.147, f32[512,32]{0,1:T(8,128)S(1)} %copy-done.22, f32[32,64,128]{2,1,0:T(8,128)S(1)} %fusion.27, f32[32,64,128]{2,1,0:T(8,128)S(1)} %bitcast.135, f32[32]{0:T(128)} %copy-done.29), kind=kOutput, calls=%fused_computation.56 | convolution fusion | flops 1613234176 | bytes 4522112 | tf_op jit(solution)/shard_map/ihp,hpn->in/dot_general | solution.py:161
  228.6 7.6 %convolution_bitcast_fusion.1 = f32[512,128]{1,0:T(8,128)} fusion(f32[512,32,64]{0,2,1:T(8,128)S(1)} %bitcast.152, f32[32,64,128]{2,1,0:T(8,128)S(1)} %bitcast.136), kind=kOutput, calls=%fused_computation.54 | convolution fusion | flops 1610612736 | bytes 5505024 | tf_op jit(solution)/shard_map/ihp,hpn->in/dot_general | solution.py:161
  236.2 3.8 fusion.51
  240.1 28.4 %all-gather.6.cloned.1.call-done = f32[32,32,8192]{2,1,0:T(8,128)} async-done(((f32[1,32,8192]{2,1,0:T(8,128)}), f32[32,32,8192]{2,1,0:T(8,128)}) %all-gather.6.cloned.1.call-update) | async-done | bytes 33554448 | tf_op jit(solution)/shard_map/all_gather | solution.py:15
  270.3 3.0 bitcast_multiply_fusion.4
  273.5 6.8 %fusion.44 = f32[512,128]{1,0:T(8,128)S(1)} fusion(bf16[512,32,64]{0,2,1:T(8,128)(2,1)S(1)} %bitcast.144, f32[512,32]{0,1:T(8,128)S(1)} %copy-done.23, f32[32,64,128]{2,1,0:T(8,128)S(1)} %copy-done.9, f32[32,64,128]{2,1,0:T(8,128)S(1)} %bitcast.154, f32[32]{0:T(128)S(1)} %copy-done.32), kind=kOutput, calls=%fused_computation.55 | convolution fusion | flops 1613234176 | bytes 4522112 | tf_op jit(solution)/shard_map/shp,hpn->sn/dot_general | solution.py:165
  283.4 7.0 %convolution_bitcast_fusion = f32[512,128]{1,0:T(8,128)S(1)} fusion(f32[512,32,64]{0,2,1:T(8,128)S(1)} %bitcast.151, f32[32,64,128]{2,1,0:T(8,128)S(1)} %bitcast.155), kind=kOutput, calls=%fused_computation.53 | convolution fusion | flops 1610612736 | bytes 5505024 | tf_op jit(solution)/shard_map/shp,hpn->sn/dot_general | solution.py:165
  293.5 22.8 %fusion.15 = bf16[512,32,64]{0,2,1:T(8,128)(2,1)} fusion(f32[32,64,512]{2,1,0:T(8,128)} %fusion.51, bf16[512,32,64]{0,2,1:T(8,128)(2,1)S(1)} %bitcast.145, f32[32,512]{1,0:T(8,128)} %copy-done.28, f32[512,512]{1,0:T(8,128)} %fusion.58, pred[512,512]{1,0:T(8,128)(4,1)} %copy-done.24, f32[512,32]{0,1:T(8,128)S(1)} %get-tuple-element.160), kind=kOutput, calls=%fused_computation.29 | convolution fusion | flops 6470762496 | bytes 9830400 | tf_op jit(solution)/shard_map/hsi,shp->ihp/dot_general | solution.py:74
  318.0 5.1 fusion.49
  323.1 22.6 %fusion.17 = bf16[512,32,64]{0,2,1:T(8,128)(2,1)} fusion(f32[32,64,512]{2,1,0:T(8,128)} %fusion.49, bf16[512,32,64]{0,2,1:T(8,128)(2,1)S(1)} %bitcast.141, f32[32,512]{1,0:T(8,128)S(1)} %copy-done.27, f32[512,512]{1,0:T(8,128)} %fusion.63, pred[512,512]{1,0:T(8,128)(4,1)} %copy-done.24, f32[512,32]{0,1:T(8,128)S(1)} %copy-done.22), kind=kOutput, calls=%fused_computation.32 | convolution fusion | flops 6470762496 | bytes 9830400 | tf_op jit(solution)/shard_map/hsi,shp->ihp/dot_general | solution.py:74
  345.7 2.9 copy.57
  348.6 4.0 copy.56
  352.6 4.1 pad_maximum_fusion
  356.7 121.6 %all-reduce.5.cloned.1.call-done = f32[32,8192]{1,0:T(8,128)} async-done(((f32[32,8192]{1,0:T(8,128)}), f32[32,8192]{1,0:T(8,128)}) %all-reduce.5.cloned.1.call-update) | async-done | bytes 1048592 | tf_op jit(solution)/shard_map/psum | solution.py:120
  478.3 48.5 %all-reduce.7.cloned.1.call-done = (f32[1024,128]{1,0:T(8,128)}, f32[1024,128]{1,0:T(8,128)}) async-done(((f32[1024,128]{1,0:T(8,128)}, f32[1024,128]{1,0:T(8,128)}), (f32[1024,128]{1,0:T(8,128)}, f32[1024,128]{1,0:T(8,128)})) %all-reduce.7.cloned.1.call-update) | async-done | bytes 1048592 | tf_op jit(solution)/shard_map/psum | solution.py:170
  (180 shorter events, 78.6 us)
Async XLA Ops:
  7.2 163.4 %all-gather.4.cloned.1.call-start = ((), (), s32[]{:S(2)}) async-start(), calls=%async_computation | async-start | bytes 34603008 | tf_op jit(solution)/shard_map/all_gather | solution.py:15
  9.6 8.5 %copy-start.25 = (f32[32,512]{1,0:T(8,128)}, f32[32,512]{1,0:T(8,128)S(1)}, u32[]{:S(2)}) copy-start(f32[32,512]{1,0:T(8,128)S(1)} %copy_bitcast_fusion.1) | copy-start | bytes 196612
  11.1 7.1 %copy-start.28 = (f32[32,512]{1,0:T(8,128)}, f32[32,512]{1,0:T(8,128)S(1)}, u32[]{:S(2)}) copy-start(f32[32,512]{1,0:T(8,128)S(1)} %copy_bitcast_fusion) | copy-start | bytes 196612
  12.5 40.4 %copy-start.29 = (f32[32]{0:T(128)}, f32[32]{0:T(128)S(1)}, u32[]{:S(2)}) copy-start(f32[32]{0:T(128)S(1)} %get-tuple-element.166) | copy-start | bytes 388
  13.3 16.2 %copy-start.31 = (f32[32]{0:T(128)}, f32[32]{0:T(128)S(1)}, u32[]{:S(2)}) copy-start(f32[32]{0:T(128)S(1)} %get-tuple-element.165) | copy-start | bytes 388
  18.1 7.6 %copy-start.14 = (bf16[1024,128]{1,0:T(8,128)(2,1)S(1)}, bf16[1024,128]{1,0:T(8,128)(2,1)}, u32[]{:S(2)}) copy-start(bf16[1024,128]{1,0:T(8,128)(2,1)} %param.12) | copy-start | bytes 786436
  21.1 137.8 %copy-start = (bf16[512,2048]{0,1:T(8,128)(2,1)}, bf16[512,2048]{0,1:T(8,128)(2,1)S(1)}, u32[]{:S(2)}) copy-start(bf16[512,2048]{0,1:T(8,128)(2,1)S(1)} %copy.60) | copy-start | bytes 6291460
  29.5 189.9 %copy-start.5 = (f32[32,64,128]{2,1,0:T(8,128)}, f32[32,64,128]{2,1,0:T(8,128)S(1)}, u32[]{:S(2)}) copy-start(f32[32,64,128]{2,1,0:T(8,128)S(1)} %fusion.27) | copy-start | bytes 3145732
  35.9 232.6 %all-gather.6.cloned.1.call-start = ((), (), s32[]{:S(2)}) async-start(), calls=%async_computation.1 | async-start | bytes 34603008 | tf_op jit(solution)/shard_map/all_gather | solution.py:15
  41.0 7.9 %copy-start.13 = (bf16[1024,128]{1,0:T(8,128)(2,1)S(1)}, bf16[1024,128]{1,0:T(8,128)(2,1)}, u32[]{:S(2)}) copy-start(bf16[1024,128]{1,0:T(8,128)(2,1)} %param.11) | copy-start | bytes 786436
  61.2 417.1 %all-reduce.5.cloned.1.call-start = ((), (), s32[]{:S(2)}) async-start(), calls=%async_computation.2 | async-start | bytes 2097152 | tf_op jit(solution)/shard_map/psum | solution.py:120
  140.4 18.5 %copy-start.24 = (pred[512,512]{1,0:T(8,128)(4,1)}, pred[512,512]{1,0:T(8,128)(4,1)S(1)}, u32[]{:S(2)}) copy-start(pred[512,512]{1,0:T(8,128)(4,1)S(1)} %iota_compare_fusion) | copy-start | bytes 786436
  144.9 14.0 %copy-start.4 = (bf16[512,2048]{0,1:T(8,128)(2,1)S(1)}, bf16[512,2048]{0,1:T(8,128)(2,1)}, u32[]{:S(2)}) copy-start(bf16[512,2048]{0,1:T(8,128)(2,1)} %copy.58) | copy-start | bytes 6291460
  144.9 14.0 %copy-start.26 = (f32[32,512]{1,0:T(8,128)S(1)}, f32[32,512]{1,0:T(8,128)}, u32[]{:S(2)}) copy-start(f32[32,512]{1,0:T(8,128)} %copy-done.25) | copy-start | bytes 196612
  170.6 48.8 %copy-start.22 = (f32[512,32]{0,1:T(8,128)S(1)}, f32[512,32]{0,1:T(8,128)}, u32[]{:S(2)}) copy-start(f32[512,32]{0,1:T(8,128)} %get-tuple-element.158) | copy-start | bytes 196612
  219.2 9.4 %copy-start.7 = (f32[512,2048]{0,1:T(8,128)S(1)}, f32[512,2048]{0,1:T(8,128)}, u32[]{:S(2)}) copy-start(f32[512,2048]{0,1:T(8,128)} %bitcast_multiply_fusion.1) | copy-start | bytes 12582916
  269.1 4.4 copy-start.2
  273.3 7.0 %copy-start.12 = (f32[512,512]{1,0:T(8,128)S(1)}, f32[512,512]{1,0:T(8,128)}, u32[]{:S(2)}) copy-start(f32[512,512]{1,0:T(8,128)} %multiply_reduce_fusion) | copy-start | bytes 3145732
  273.3 7.0 %copy-start.15 = (bf16[1024,128]{1,0:T(8,128)(2,1)S(1)}, bf16[1024,128]{1,0:T(8,128)(2,1)}, u32[]{:S(2)}) copy-start(bf16[1024,128]{1,0:T(8,128)(2,1)} %param.12) | copy-start | bytes 786436
  273.3 7.0 %copy-start.21 = (f32[512,128]{1,0:T(8,128)S(1)}, f32[512,128]{1,0:T(8,128)}, u32[]{:S(2)}) copy-start(f32[512,128]{1,0:T(8,128)} %convolution_bitcast_fusion.1) | copy-start | bytes 786436
  273.5 9.9 %copy-start.6 = (f32[512,2048]{0,1:T(8,128)S(1)}, f32[512,2048]{0,1:T(8,128)}, u32[]{:S(2)}) copy-start(f32[512,2048]{0,1:T(8,128)} %bitcast_multiply_fusion) | copy-start | bytes 12582916
  280.3 10.0 %copy-start.11 = (f32[512,512]{1,0:T(8,128)S(1)}, f32[512,512]{1,0:T(8,128)}, u32[]{:S(2)}) copy-start(f32[512,512]{1,0:T(8,128)} %multiply_reduce_fusion.1) | copy-start | bytes 3145732
  280.3 10.0 %copy-start.16 = (f32[512,128]{1,0:T(8,128)S(1)}, f32[512,128]{1,0:T(8,128)}, u32[]{:S(2)}) copy-start(f32[512,128]{1,0:T(8,128)} %fusion.45) | copy-start | bytes 786436
  283.4 10.1 %copy-start.3 = (bf16[512,2048]{0,1:T(8,128)(2,1)S(1)}, bf16[512,2048]{0,1:T(8,128)(2,1)}, u32[]{:S(2)}) copy-start(bf16[512,2048]{0,1:T(8,128)(2,1)} %copy.53) | copy-start | bytes 6291460
  293.4 24.6 %copy-start.30 = (f32[32]{0:T(128)S(1)}, f32[32]{0:T(128)}, u32[]{:S(2)}) copy-start(f32[32]{0:T(128)} %copy-done.29) | copy-start | bytes 388
  293.4 233.3 %all-reduce.7.cloned.1.call-start = ((), (), s32[]{:S(2)}) async-start(), calls=%async_computation.3 | async-start | bytes 2097152 | tf_op jit(solution)/shard_map/psum | solution.py:170
  293.5 22.8 %copy-start.18 = (f32[512,128]{1,0:T(8,128)S(1)}, f32[512,128]{1,0:T(8,128)}, u32[]{:S(2)}) copy-start(f32[512,128]{1,0:T(8,128)} %convolution_add_fusion.2) | copy-start | bytes 786436
  293.5 22.8 %copy-start.20 = (f32[512,128]{1,0:T(8,128)S(1)}, f32[512,128]{1,0:T(8,128)}, u32[]{:S(2)}) copy-start(f32[512,128]{1,0:T(8,128)} %convolution_add_fusion.3) | copy-start | bytes 786436
  293.5 23.7 %copy-start.17 = (f32[512,128]{1,0:T(8,128)S(1)}, f32[512,128]{1,0:T(8,128)}, u32[]{:S(2)}) copy-start(f32[512,128]{1,0:T(8,128)} %convolution_add_fusion) | copy-start | bytes 786436
  293.5 23.6 %copy-start.19 = (f32[512,128]{1,0:T(8,128)S(1)}, f32[512,128]{1,0:T(8,128)}, u32[]{:S(2)}) copy-start(f32[512,128]{1,0:T(8,128)} %convolution_add_fusion.1) | copy-start | bytes 786436
  317.2 5.9 %copy-start.1 = (bf16[512,2048]{0,1:T(8,128)(2,1)S(1)}, bf16[512,2048]{0,1:T(8,128)(2,1)}, u32[]{:S(2)}) copy-start(bf16[512,2048]{0,1:T(8,128)(2,1)} %copy-done) | copy-start | bytes 6291460
  317.2 6.0 %copy-start.27 = (f32[32,512]{1,0:T(8,128)S(1)}, f32[32,512]{1,0:T(8,128)}, u32[]{:S(2)}) copy-start(f32[32,512]{1,0:T(8,128)} %copy-done.25) | copy-start | bytes 196612
  (6 other events, 17.9 us)
Sparse Core Ops, SparseCore 0:
  36.0 117.0 all-gather.3
  155.4 113.0 all-gather.5
  293.5 184.7 all-reduce.4
  481.3 45.4 all-reduce.6
where the time goes:
time: 547 us; the launch traced here: 540 us
  waiting for transfers between devices  199 us (36%)
  matrix products  137 us (25%)
  blocking collectives  70.5 us (13%)
  other arithmetic  67.2 us (12%)
  local copies, waits for them, and re-layouts  48.8 us (9%)
  between operations  15.3 us (3%)
    psum x1, waiting for transfers between devices, per_device(): initial_grad = lax.psum(jnp.exp(prefix_log) * local_adjoint, 'seq')  122 us
    unnamed x1, blocking collectives  70.5 us
    psum x1, waiting for transfers between devices, per_device(): writes_grad, reads_grad = lax.psum((writes_local, reads_local), 'head')  48.5 us
    add x31, other arithmetic, backward_join(): return (earlier[0] + latter[0], latter[1] + jnp.exp(latter[0]) * earlier[1])  46.8 us
    dot_general x2, matrix products, per_device(): jnp.einsum('hsi,shp->ihp', intersections[None] * decay_mask, grads_wide,...  45.4 us
    all_gather x2, waiting for transfers between devices, carried_in(): gathered = jax.tree.map(lambda a: lax.all_gather(a, axis), part)  28.4 us
    dot_general x2, matrix products, per_device(): jnp.einsum('shp,ihp->hsi', block_grads, block_values, preferred_element_t...  25.7 us
    dot_general x2, matrix products, per_device(): jnp.einsum('ihp,hpn->in', rescaled_quantities, afters[block_index], preci...  16.8 us
  transfers between devices with their start and end apart: 4, of which 3 were waited for; matrix products, arithmetic and copies ran while one was open for 36% of the time, Pallas kernels for 0%

commit v1 on v0

--- a/solution.py
+++ b/solution.py
@@ -117,7 +117,9 @@
         (total_log[:, None], local_adjoint), "seq", backward_join, empty, True
     )
     entering = prefix_state + jnp.exp(prefix_log) * starting_head_state
-    initial_grad = lax.psum(jnp.exp(prefix_log) * local_adjoint, "seq")
+    part_2 = jnp.exp(prefix_log) * local_adjoint
+    parts = lax.all_gather(part_2, "seq", axis=0, tiled=False)
+    initial_grad = parts.sum(axis=0)
     start_state = entering.reshape(state_shape)
     starts = []
     for block_index in range(block_count):

time: 547 us -> 446 us (0.82)
  waiting for transfers between devices: 199 us -> 105 us
  matrix products: 137 us -> 124 us
  other arithmetic: 67.2 us -> 80 us
  local copies, waits for them, and re-layouts: 48.8 us -> 42.1 us
    psum x1 -> x0, waiting for transfers between devices: 122 us -> none  [per_device(): initial_grad = lax.psum(jnp.exp(prefix_log) * local_adjoint, 'seq')]
    all_gather x2, waiting for transfers between devices: 28.4 us -> 98.4 us  [carried_in(): gathered = jax.tree.map(lambda a: lax.all_gather(a, axis), part)]
    psum x1, waiting for transfers between devices: 48.5 us -> 6.18 us  [per_device(): writes_grad, reads_grad = lax.psum((writes_local, reads_local), 'head')]
    reduce_sum x0 -> x1, other arithmetic: none -> 12.8 us  [per_device(): initial_grad = parts.sum(axis=0)]
    unnamed x79 -> x86, local copies, waits for them, and re-layouts: 16.6 us -> 14.4 us
  transfers between devices with their start and end apart: 4 -> 4, of which waited for: 3 -> 3; matrix products, arithmetic and copies ran while one was open for 36% -> 50% of each run, Pallas kernels for 0% -> 0%
where the time goes in v1:
time: 446 us; the launch traced here: 438 us
  matrix products  124 us (28%)
  waiting for transfers between devices  105 us (24%)
  other arithmetic  80 us (18%)
  blocking collectives  69.7 us (16%)
  local copies, waits for them, and re-layouts  42.1 us (9%)
  between operations  15.5 us (3%)
    all_gather x2, waiting for transfers between devices, carried_in(): gathered = jax.tree.map(lambda a: lax.all_gather(a, axis), part)  98.4 us
    unnamed x1, blocking collectives  69.7 us
    add x31, other arithmetic, backward_join(): return (earlier[0] + latter[0], latter[1] + jnp.exp(latter[0]) * earlier[1])  46.4 us
    dot_general x2, matrix products, per_device(): jnp.einsum('hsi,shp->ihp', intersections[None] * decay_mask, grads_wide,...  44.2 us
    dot_general x2, matrix products, per_device(): jnp.einsum('shp,ihp->hsi', block_grads, block_values, preferred_element_t...  25.3 us
    unnamed x86, local copies, waits for them, and re-layouts  14.4 us
    dot_general x2, matrix products, per_device(): jnp.einsum('shp,hpn->sn', scaled_grads, starts[block_index], precision=hi...  13.7 us
    dot_general x2, matrix products, per_device(): jnp.einsum('ihp,hpn->in', rescaled_quantities, afters[block_index], preci...  13.7 us
  transfers between devices with their start and end apart: 4, of which 3 were waited for; matrix products, arithmetic and copies ran while one was open for 50% of the time, Pallas kernels for 0%

profile of v1, /device:TPU:0, one launch (start us, length us, event | category | flops | bytes accessed | tf_op | source)
XLA Modules:
  0.0 437.9 jit_solution(11163015666870122676)
XLA Ops:
  12.7 4.0 fusion.75
  16.7 2.6 copy.61
  19.3 2.9 copy.58
  22.2 2.3 fusion.21
  25.5 3.8 fusion.41
  30.8 4.8 %fusion.76 = (bf16[512,2048]{1,0:T(8,128)(2,1)}, bf16[512,2048]{1,0:T(8,128)(2,1)}) fusion(bf16[1024,2048]{1,0:T(8,128)(2,1)} %param.13), kind=kLoop, calls=%fused_computation.117 | loop fusion | bytes 8388608 | tf_op jit(solution)/shard_map/slice | solution.py:51
  35.7 2.9 copy.60
  38.6 4.6 %copy.53 = bf16[512,2048]{0,1:T(8,128)(2,1)} copy(bf16[512,2048]{1,0:T(8,128)(2,1)} %get-tuple-element.154) | data formatting | bytes 4194304 | tf_op jit(solution)/shard_map/slice | solution.py:51
  43.2 4.1 fusion.27
  48.3 3.2 fusion.38
  54.2 69.7 %all-reduce = f32[1024]{0:T(1024)S(1)} all-reduce(f32[1024]{0:T(1024)S(1)} %dynamic-update-slice), channel_id=2, replica_groups=mesh['seq'=32,'head'=4] {'seq'}, use_global_device_ids=true, to_apply=%add | all-reduce | flops 1024 | bytes 8192
  123.9 23.8 %all-gather.7.cloned.1.call-done = f32[32,32,8192]{2,1,0:T(8,128)} async-done(((f32[1,32,8192]{2,1,0:T(8,128)}), f32[32,32,8192]{2,1,0:T(8,128)}) %all-gather.7.cloned.1.call-update) | async-done | bytes 33554448 | tf_op jit(solution)/shard_map/all_gather | solution.py:15
  149.6 2.4 broadcast_multiply_fusion
  152.3 4.2 bitcast_multiply_fusion.1
  156.5 2.6 bitcast_multiply_fusion
  159.2 2.3 fusion.58
  163.7 13.7 %multiply_reduce_fusion = f32[512,512]{1,0:T(8,128)} fusion(f32[32,512]{1,0:T(8,128)} %copy-done.29, pred[512,512]{1,0:T(8,128)(4,1)S(1)} %iota_compare_fusion, bf16[512,32,64]{0,2,1:T(8,128)(2,1)} %bitcast.140, bf16[512,32,64]{0,2,1:T(8,128)(2,1)} %bitcast.147), kind=kOutput, calls=%fused_computation.6 | convolution fusion | flops 1107034112 | bytes 5570560 | tf_op jit(solution)/shard_map/shp,ihp->hsi/dot_general | solution.py:66
  177.4 11.7 %multiply_reduce_fusion.1 = f32[512,512]{1,0:T(8,128)} fusion(f32[32,512]{1,0:T(8,128)S(1)} %copy-done.28, pred[512,512]{1,0:T(8,128)(4,1)S(1)} %iota_compare_fusion, bf16[512,32,64]{0,2,1:T(8,128)(2,1)S(1)} %bitcast.137, bf16[512,32,64]{0,2,1:T(8,128)(2,1)S(1)} %bitcast.144), kind=kOutput, calls=%fused_computation.7 | convolution fusion | flops 1107034112 | bytes 5570560 | tf_op jit(solution)/shard_map/shp,ihp->hsi/dot_general | solution.py:66
  189.1 74.6 %all-gather.5.cloned.1.call-done = f32[32,32,8192]{2,1,0:T(8,128)} async-done(((f32[1,32,8192]{2,1,0:T(8,128)}), f32[32,32,8192]{2,1,0:T(8,128)}) %all-gather.5.cloned.1.call-update) | async-done | bytes 33554448 | tf_op jit(solution)/shard_map/all_gather | solution.py:15
  263.8 48.2 %while.26 = (s32[]{:T(128)}, f32[32,8192]{1,0:T(8,128)S(1)}, s32[]{:T(128)}, f32[32,32,8192]{2,1,0:T(8,128)}, f32[32,32,1]{1,2,0:T(1,128)S(1)}, /*index=5*/s32[]{:T(128)}, s32[]{:T(128)}, s32[]{:T(128)}, s32[]{:T(128)}) while((s32[]{:T(128)}, f32[32,8192]{1,0:T(8,128)S(1)}, s32[]{:T(128)}, f32[32,32,8192]{2,1,0:T(8,128)}, ...), condition=%wide.region_5.6_spmd, body=%wide.region_4.5_spmd.sunk | while | flops 524294 | bytes 3146267 | solution.py:24
  314.5 6.8 %convolution_bitcast_fusion.1 = f32[512,128]{1,0:T(8,128)S(1)} fusion(f32[512,32,64]{0,2,1:T(8,128)S(1)} %bitcast.149, f32[32,64,128]{2,1,0:T(8,128)S(1)} %bitcast.132), kind=kOutput, calls=%fused_computation.54 | convolution fusion | flops 1610612736 | bytes 5505024 | tf_op jit(solution)/shard_map/ihp,hpn->in/dot_general | solution.py:163
  322.4 6.9 %fusion.45 = f32[512,128]{1,0:T(8,128)S(1)} fusion(bf16[512,32,64]{0,2,1:T(8,128)(2,1)S(1)} %bitcast.145, f32[512,32]{0,1:T(8,128)S(1)} %copy-done.21, f32[32,64,128]{2,1,0:T(8,128)S(1)} %copy-done.8, f32[32,64,128]{2,1,0:T(8,128)S(1)} %bitcast.133, f32[32]{0:T(128)S(1)} %copy-done.32), kind=kOutput, calls=%fused_computation.56 | convolution fusion | flops 1613234176 | bytes 4522112 | tf_op jit(solution)/shard_map/ihp,hpn->in/dot_general | solution.py:163
  331.2 6.8 %fusion.44 = f32[512,128]{1,0:T(8,128)S(1)} fusion(bf16[512,32,64]{0,2,1:T(8,128)(2,1)S(1)} %bitcast.141, f32[512,32]{0,1:T(8,128)S(1)} %copy-done.23, f32[32,64,128]{2,1,0:T(8,128)S(1)} %copy-done.12, f32[32,64,128]{2,1,0:T(8,128)S(1)} %bitcast.150, f32[32]{0:T(128)S(1)} %copy-done.34), kind=kOutput, calls=%fused_computation.55 | convolution fusion | flops 1613234176 | bytes 4522112 | tf_op jit(solution)/shard_map/shp,hpn->sn/dot_general | solution.py:167
  338.6 7.0 %convolution_bitcast_fusion = f32[512,128]{1,0:T(8,128)S(1)} fusion(f32[512,32,64]{0,2,1:T(8,128)S(1)} %bitcast.148, f32[32,64,128]{2,1,0:T(8,128)S(1)} %bitcast.151), kind=kOutput, calls=%fused_computation.53 | convolution fusion | flops 1610612736 | bytes 5505024 | tf_op jit(solution)/shard_map/shp,hpn->sn/dot_general | solution.py:167
  348.9 3.9 fusion.49
  352.9 21.8 %fusion.15 = bf16[512,32,64]{0,2,1:T(8,128)(2,1)} fusion(f32[32,64,512]{2,1,0:T(8,128)S(1)} %fusion.51, bf16[512,32,64]{0,2,1:T(8,128)(2,1)S(1)} %bitcast.142, f32[32,512]{1,0:T(8,128)S(1)} %copy-done.30, f32[512,512]{1,0:T(8,128)S(1)} %copy-done.19, pred[512,512]{1,0:T(8,128)(4,1)S(1)} %copy-done.25, f32[512,32]{0,1:T(8,128)S(1)} %get-tuple-element.160), kind=kOutput, calls=%fused_computation.29 | convolution fusion | flops 6470762496 | bytes 9830400 | tf_op jit(solution)/shard_map/hsi,shp->ihp/dot_general | solution.py:74
  374.7 22.4 %fusion.17 = bf16[512,32,64]{0,2,1:T(8,128)(2,1)} fusion(f32[32,64,512]{2,1,0:T(8,128)} %fusion.49, bf16[512,32,64]{0,2,1:T(8,128)(2,1)S(1)} %bitcast.138, f32[32,512]{1,0:T(8,128)} %copy-done.27, f32[512,512]{1,0:T(8,128)S(1)} %copy-done.18, pred[512,512]{1,0:T(8,128)(4,1)S(1)} %copy-done.26, f32[512,32]{0,1:T(8,128)S(1)} %copy-done.21), kind=kOutput, calls=%fused_computation.32 | convolution fusion | flops 6470762496 | bytes 9830400 | tf_op jit(solution)/shard_map/hsi,shp->ihp/dot_general | solution.py:74
  397.1 2.9 copy.57
  400.1 4.0 copy.56
  404.0 4.1 pad_maximum_fusion
  408.2 12.8 %reduce_sum.29 = f32[32,8192]{1,0:T(8,128)} reduce(f32[32,32,8192]{2,1,0:T(8,128)} %all-gather.9.cloned.1.call-done, f32[]{:T(128)} %constant.59.clone.1), dimensions={0}, to_apply=%region_12.13 | reduce | flops 8126464 | bytes 34603012 | tf_op jit(solution)/shard_map/reduce_sum | solution.py:122
  421.0 6.2 %all-reduce.4.cloned.1.call-done = (f32[1024,128]{1,0:T(8,128)}, f32[1024,128]{1,0:T(8,128)}) async-done(((f32[1024,128]{1,0:T(8,128)}, f32[1024,128]{1,0:T(8,128)}), (f32[1024,128]{1,0:T(8,128)}, f32[1024,128]{1,0:T(8,128)})) %all-reduce.4.cloned.1.call-update) | async-done | bytes 1048592 | tf_op jit(solution)/shard_map/psum | solution.py:172
  (189 shorter events, 75.4 us)
Async XLA Ops:
  7.2 140.6 %all-gather.7.cloned.1.call-start = ((), (), s32[]{:S(2)}) async-start(), calls=%async_computation.1 | async-start | bytes 34603008 | tf_op jit(solution)/shard_map/all_gather | solution.py:15
  12.0 12.4 %copy-start.31 = (f32[32]{0:T(128)}, f32[32]{0:T(128)S(1)}, u32[]{:S(2)}) copy-start(f32[32]{0:T(128)S(1)} %get-tuple-element.164) | copy-start | bytes 388
  12.2 10.0 %copy-start.20 = (f32[512,32]{0,1:T(8,128)}, f32[512,32]{0,1:T(8,128)S(1)}, u32[]{:S(2)}) copy-start(f32[512,32]{0,1:T(8,128)S(1)} %get-tuple-element.158) | copy-start | bytes 196612
  12.7 34.6 %copy-start.33 = (f32[32]{0:T(128)}, f32[32]{0:T(128)S(1)}, u32[]{:S(2)}) copy-start(f32[32]{0:T(128)S(1)} %get-tuple-element.163) | copy-start | bytes 388
  16.7 5.4 %copy-start.15 = (bf16[1024,128]{1,0:T(8,128)(2,1)S(1)}, bf16[1024,128]{1,0:T(8,128)(2,1)}, u32[]{:S(2)}) copy-start(bf16[1024,128]{1,0:T(8,128)(2,1)} %param.11) | copy-start | bytes 786436
  22.1 8.4 %copy-start.4 = (bf16[512,2048]{0,1:T(8,128)(2,1)}, bf16[512,2048]{0,1:T(8,128)(2,1)S(1)}, u32[]{:S(2)}) copy-start(bf16[512,2048]{0,1:T(8,128)(2,1)S(1)} %copy.58) | copy-start | bytes 6291460
  30.6 233.1 %all-gather.5.cloned.1.call-start = ((), (), s32[]{:S(2)}) async-start(), calls=%async_computation | async-start | bytes 34603008 | tf_op jit(solution)/shard_map/all_gather | solution.py:15
  35.6 7.6 %copy-start.16 = (bf16[1024,128]{1,0:T(8,128)(2,1)S(1)}, bf16[1024,128]{1,0:T(8,128)(2,1)}, u32[]{:S(2)}) copy-start(bf16[1024,128]{1,0:T(8,128)(2,1)} %param.12) | copy-start | bytes 786436
  35.6 7.6 %copy-start.22 = (f32[512,32]{0,1:T(8,128)S(1)}, f32[512,32]{0,1:T(8,128)}, u32[]{:S(2)}) copy-start(f32[512,32]{0,1:T(8,128)} %get-tuple-element.161) | copy-start | bytes 196612
  38.6 138.8 %copy-start = (bf16[512,2048]{0,1:T(8,128)(2,1)}, bf16[512,2048]{0,1:T(8,128)(2,1)S(1)}, u32[]{:S(2)}) copy-start(bf16[512,2048]{0,1:T(8,128)(2,1)S(1)} %copy.60) | copy-start | bytes 6291460
  47.3 5.4 %copy-start.37 = (u32[128]{0:T(128)S(1)}, u32[128]{0:T(128)}, u32[]{:S(2)}) copy-start(u32[128]{0:T(128)} %constant.67) | copy-start | bytes 1540
  52.6 355.5 %all-gather.9.cloned.1.call-start = ((), (), s32[]{:S(2)}) async-start(), calls=%async_computation.2 | async-start | bytes 34603008 | tf_op jit(solution)/shard_map/all_gather | solution.py:121
  152.0 275.1 %all-reduce.4.cloned.1.call-start = ((), (), s32[]{:S(2)}) async-start(), calls=%async_computation.3 | async-start | bytes 2097152 | tf_op jit(solution)/shard_map/psum | solution.py:172
  159.2 18.2 %copy-start.24 = (pred[512,512]{1,0:T(8,128)(4,1)}, pred[512,512]{1,0:T(8,128)(4,1)S(1)}, u32[]{:S(2)}) copy-start(pred[512,512]{1,0:T(8,128)(4,1)S(1)} %iota_compare_fusion) | copy-start | bytes 786436
  163.7 13.7 %copy-start.5 = (bf16[512,2048]{0,1:T(8,128)(2,1)S(1)}, bf16[512,2048]{0,1:T(8,128)(2,1)}, u32[]{:S(2)}) copy-start(bf16[512,2048]{0,1:T(8,128)(2,1)} %copy-done.4) | copy-start | bytes 6291460
  163.7 13.7 %copy-start.28 = (f32[32,512]{1,0:T(8,128)S(1)}, f32[32,512]{1,0:T(8,128)}, u32[]{:S(2)}) copy-start(f32[32,512]{1,0:T(8,128)} %copy-done.27) | copy-start | bytes 196612
  263.7 48.4 %copy-start.36 = (f32[32]{0:T(128)S(1)}, f32[32]{0:T(128)}, u32[]{:S(2)}) copy-start(f32[32]{0:T(128)} %copy-done.35) | copy-start | bytes 388
  313.7 7.5 %copy-start.14 = (f32[512,512]{1,0:T(8,128)S(1)}, f32[512,512]{1,0:T(8,128)}, u32[]{:S(2)}) copy-start(f32[512,512]{1,0:T(8,128)} %multiply_reduce_fusion) | copy-start | bytes 3145732
  313.8 7.5 %copy-start.17 = (bf16[1024,128]{1,0:T(8,128)(2,1)S(1)}, bf16[1024,128]{1,0:T(8,128)(2,1)}, u32[]{:S(2)}) copy-start(bf16[1024,128]{1,0:T(8,128)(2,1)} %param.12) | copy-start | bytes 786436
  313.8 8.6 %copy-start.6 = (bf16[512,2048]{0,1:T(8,128)(2,1)S(1)}, bf16[512,2048]{0,1:T(8,128)(2,1)}, u32[]{:S(2)}) copy-start(bf16[512,2048]{0,1:T(8,128)(2,1)} %copy-done.4) | copy-start | bytes 6291460
  313.8 8.6 %copy-start.8 = (f32[32,64,128]{2,1,0:T(8,128)S(1)}, f32[32,64,128]{2,1,0:T(8,128)}, u32[]{:S(2)}) copy-start(f32[32,64,128]{2,1,0:T(8,128)} %copy-done.7) | copy-start | bytes 3145732
  313.8 8.6 %copy-start.21 = (f32[512,32]{0,1:T(8,128)S(1)}, f32[512,32]{0,1:T(8,128)}, u32[]{:S(2)}) copy-start(f32[512,32]{0,1:T(8,128)} %copy-done.20) | copy-start | bytes 196612
  313.8 8.6 %copy-start.32 = (f32[32]{0:T(128)S(1)}, f32[32]{0:T(128)}, u32[]{:S(2)}) copy-start(f32[32]{0:T(128)} %copy-done.31) | copy-start | bytes 388
  321.3 8.1 %copy-start.13 = (f32[512,512]{1,0:T(8,128)S(1)}, f32[512,512]{1,0:T(8,128)}, u32[]{:S(2)}) copy-start(f32[512,512]{1,0:T(8,128)} %multiply_reduce_fusion.1) | copy-start | bytes 3145732
  321.3 9.9 %copy-start.2 = (bf16[512,2048]{0,1:T(8,128)(2,1)S(1)}, bf16[512,2048]{0,1:T(8,128)(2,1)}, u32[]{:S(2)}) copy-start(bf16[512,2048]{0,1:T(8,128)(2,1)} %copy.53) | copy-start | bytes 6291460
  321.3 9.9 %copy-start.12 = (f32[32,64,128]{2,1,0:T(8,128)S(1)}, f32[32,64,128]{2,1,0:T(8,128)}, u32[]{:S(2)}) copy-start(f32[32,64,128]{2,1,0:T(8,128)} %copy-done.11) | copy-start | bytes 3145732
  321.3 9.9 %copy-start.23 = (f32[512,32]{0,1:T(8,128)S(1)}, f32[512,32]{0,1:T(8,128)}, u32[]{:S(2)}) copy-start(f32[512,32]{0,1:T(8,128)} %get-tuple-element.161) | copy-start | bytes 196612
  321.3 9.9 %copy-start.34 = (f32[32]{0:T(128)S(1)}, f32[32]{0:T(128)}, u32[]{:S(2)}) copy-start(f32[32]{0:T(128)} %copy-done.33) | copy-start | bytes 388
  329.3 9.3 %copy-start.9 = (f32[512,2048]{0,1:T(8,128)S(1)}, f32[512,2048]{0,1:T(8,128)}, u32[]{:S(2)}) copy-start(f32[512,2048]{0,1:T(8,128)} %bitcast_multiply_fusion) | copy-start | bytes 12582916
  352.8 21.8 %copy-start.1 = (bf16[512,2048]{0,1:T(8,128)(2,1)S(1)}, bf16[512,2048]{0,1:T(8,128)(2,1)}, u32[]{:S(2)}) copy-start(bf16[512,2048]{0,1:T(8,128)(2,1)} %copy-done) | copy-start | bytes 6291460
  352.8 21.8 %copy-start.18 = (f32[512,512]{1,0:T(8,128)S(1)}, f32[512,512]{1,0:T(8,128)}, u32[]{:S(2)}) copy-start(f32[512,512]{1,0:T(8,128)} %fusion.63) | copy-start | bytes 3145732
  352.8 21.8 %copy-start.26 = (pred[512,512]{1,0:T(8,128)(4,1)S(1)}, pred[512,512]{1,0:T(8,128)(4,1)}, u32[]{:S(2)}) copy-start(pred[512,512]{1,0:T(8,128)(4,1)} %copy-done.24) | copy-start | bytes 786436
  (10 other events, 24.3 us)
Sparse Core Ops, SparseCore 0:
  30.7 117.0 all-gather.6
  150.6 113.0 all-gather.4
  265.9 113.1 all-gather.8
  382.0 45.0 all-reduce.3
